TPU v7x, 32 devices: a whole 2x2x4 slice. The times are simulated.
32 devices in a mesh: gx: 8 (over z, x), gy: 4 (over y, core).
Axes of the slice: x: 2, y: 2, z: 4, core: 2. Of those that a mesh axis runs over, the one named last changes fastest.
Arguments:
- hydro: float32 [192, 192, 792], P('gx', 'gy'), may hold values from 0.05 to 2
- winds: float32 [192, 192, 24], P('gx', 'gy'), may hold values from -0.3 to 0.3
- cloud_mask: int32 [192, 192], P('gx', 'gy'), may hold values from 0 to 1, as said below
- coal_kernel: bfloat16 [4356, 66], replicated, may hold values from -0.09375 to 0.09375
- block_mask: int32 [6, 6], replicated, may hold values 0 or 1
Outputs:
- hydro_next: float32 [192, 192, 792], P('gx', 'gy')
Inputs may be any that keep to these rules, and one draw needn't show every extreme that they name: `cloud_mask`: exactly 4608 columns are cloudy; the columns of one aligned tile of 24 x 48 are all cloudy.
All inputs are finite; a program needn't handle non-finite values.
Results may differ from a plain program's by a relative error of at most 0.0017.
Values may be sent and summed in bfloat16 or wider, within the bound.
A program may use at most 128 MiB of HBM per device.

v0:
```python
import jax
import jax.numpy as jnp
from jax import lax
from jax.sharding import PartitionSpec as P

BLK = 11


def padded_2(array, sides, width):
    for axis, dim in sides:
        count, length = (lax.axis_size(axis), array.shape[dim])
        up = [(i, (i + 1) % count) for i in range(count)]
        down = [(j, i) for i, j in up]
        last = lax.slice_in_dim(array, length - width, length, axis=dim)
        initial = lax.slice_in_dim(array, 0, width, axis=dim)
        before = lax.ppermute(last, axis, up)
        after = lax.ppermute(initial, axis, down)
        array = jnp.concatenate([before, array, after], axis=dim)
    return array


def coalesce(rows2d, chan, kernel_wide):
    total = rows2d.shape[0] * (rows2d.shape[1] // chan)
    cells = rows2d.reshape(total, chan)
    pieces = 1
    while total % pieces != 0 or total // pieces > 2048:
        pieces = pieces + 1

    def one_block(block):
        wide = block.astype(jnp.float32)
        pairs = (wide[:, :, None] * wide[:, None, :]).astype(jnp.bfloat16).reshape(-1, chan * chan)
        return jnp.dot(pairs, kernel_wide, preferred_element_type=jnp.float32).astype(jnp.bfloat16)

    result = lax.map(one_block, cells.reshape(pieces, total // pieces, chan))
    result = result.reshape(total, kernel_wide.shape[1])[:, :chan]
    return result.reshape(rows2d.shape[0], rows2d.shape[1])


def per_device(hydro, winds, cloud_mask, coal_kernel, block_mask):
    size_x, size_y, width = hydro.shape
    levels = winds.shape[2] // 2
    chan = width // levels
    stacked = jnp.concatenate([hydro, winds], axis=2)
    padded = padded_2(stacked, (("gx", 0), ("gy", 1)), 1)
    field = padded[:, :, :width]
    wind_x = padded[:, :, width : width + levels]
    wind_y = padded[:, :, width + levels :]
    along_x = field[:, 1:-1]
    face_x = jnp.repeat(0.5 * (wind_x[:-1, 1:-1] + wind_x[1:, 1:-1]), chan, axis=2)
    flux_x = jnp.maximum(face_x, 0.0) * along_x[:-1] + jnp.minimum(face_x, 0.0) * along_x[1:]
    along_y = field[1:-1]
    face_y = jnp.repeat(0.5 * (wind_y[1:-1, :-1] + wind_y[1:-1, 1:]), chan, axis=2)
    flux_y = jnp.maximum(face_y, 0.0) * along_y[:, :-1] + jnp.minimum(face_y, 0.0) * along_y[:, 1:]
    q_adv = field[1:-1, 1:-1] - (flux_x[1:] - flux_x[:-1]) - (flux_y[:, 1:] - flux_y[:, :-1])
    blocks_count = block_mask.shape[0]
    onehot = ((jnp.arange(chan) // BLK)[:, None] == jnp.arange(blocks_count)[None, :]).astype(
        jnp.float32
    )
    blockmap = jnp.dot(jnp.dot(onehot, block_mask.astype(jnp.float32)), onehot.T)
    kernel_eff = jnp.where(
        blockmap.reshape(chan * chan, 1) > 0.5, coal_kernel, jnp.zeros_like(coal_kernel)
    )
    lanes = (chan + 127) // 128 * 128
    kernel_wide = jnp.concatenate(
        [kernel_eff, jnp.zeros((chan * chan, lanes - chan), jnp.bfloat16)], axis=1
    )
    ncols = size_x * size_y
    flat = cloud_mask.reshape(-1)
    columns = q_adv.astype(jnp.bfloat16).reshape(ncols, width)
    size_gx = lax.axis_size("gx")
    size_gy = lax.axis_size("gy")
    devices = size_gx * size_gy
    me_index = lax.axis_index("gx") * size_gy + lax.axis_index("gy")
    count = jnp.sum(flat)
    counts = lax.all_gather(count.reshape(1), ("gx", "gy"), axis=0, tiled=True)
    starts = jnp.cumsum(counts) - counts
    ends = starts + counts
    offset = starts[me_index]
    send_rows = ncols // devices
    owned = ncols // 8
    source_index = jnp.nonzero(flat, size=ncols, fill_value=0)[0].astype(jnp.int32)
    slot_pos = jnp.arange(send_rows, dtype=jnp.int32)[:, None]
    slot_dev = jnp.arange(devices, dtype=jnp.int32)[None, :]
    send_rank = (slot_pos * devices + (slot_dev - offset) % devices).reshape(-1)
    send_alive = send_rank < count
    outgoing = jnp.where(
        send_alive[:, None], columns[source_index[send_rank]], jnp.zeros((), jnp.bfloat16)
    )
    outgoing = outgoing.reshape(send_rows, devices, width)
    position = jnp.arange(send_rows)[:, None]
    rel_rank = position * devices + ((me_index - starts) % devices)[None, :]
    alive_slot = rel_rank < counts[None, :]
    slot_of = jnp.where(alive_slot, (starts[None, :] + rel_rank) // devices, owned)
    global_rank = jnp.arange(owned) * devices + me_index
    source_dev = jnp.sum((ends[None, :] <= global_rank[:, None]).astype(jnp.int32), axis=1)
    local_rank = global_rank - starts[source_dev]
    arrive_row = local_rank // devices * devices + source_dev
    arrived = lax.all_to_all(outgoing, ("gx", "gy"), split_axis=1, concat_axis=1, tiled=True)
    gathered = arrived.reshape(send_rows * devices, width)[arrive_row]
    computed = coalesce(gathered, chan, kernel_wide)
    extended = jnp.concatenate([computed, jnp.zeros((1, width), jnp.bfloat16)], axis=0)
    returned = lax.all_to_all(
        extended[slot_of.reshape(-1)].reshape(send_rows, devices, width),
        ("gx", "gy"),
        split_axis=1,
        concat_axis=1,
        tiled=True,
    )
    returned = returned.reshape(send_rows * devices, width)
    column_rank = jnp.maximum(jnp.cumsum(flat) - 1, 0)
    back_row = column_rank // devices * devices + (column_rank % devices + offset) % devices
    tendency = jnp.where(flat[:, None] > 0, returned[back_row].astype(jnp.float32), 0.0)
    result = q_adv + tendency.reshape(size_x, size_y, width)
    return result


def solution(mesh):
    in_specs = (P("gx", "gy", None), P("gx", "gy", None), P("gx", "gy"), P(), P())
    out_specs = P("gx", "gy", None)
    return jax.shard_map(
        per_device, mesh=mesh, in_specs=in_specs, out_specs=out_specs, check_vma=False
    )
```

profile of v0, /device:TPU:0, one launch (start us, length us, event | category | flops | bytes accessed | tf_op | source)
XLA Modules:
  0.0 341.7 jit_solution(962298888700188795)
XLA Ops:
  0.0 1.2 copy.91
  1.2 1.1 pad_maximum_fusion.15
  2.3 6.0 %collective-permute-start.1 = (f32[1,48,816]{2,1,0:T(8,128)S(1)}, f32[1,48,816]{2,1,0:T(8,128)S(1)}, u32[]{:S(2)}, u32[]{:S(2)}) collective-permute-start(f32[1,48,816]{2,1,0:T(8,128)S(1)} %get-tuple-element.30), channel_id=1, source_target_pairs={{4,0},{8,4},{12,8},{16,12},{20,16},{24,20},{28,24},{0,28},{5,1},{9... | collective-permute-start | bytes 470024 | tf_op jit(solution)/shard_map/ppermute | solution.py:17
  8.4 0.7 fusion.35
  9.1 0.8 dynamic-update-slice
  9.9 40.1 %all-reduce.2 = s32[32]{0:T(128)S(1)} all-reduce(s32[32]{0:T(128)S(1)} %dynamic-update-slice), channel_id=1, replica_groups=mesh['gx'=8,'gy'=4] {'gx','gy'}, use_global_device_ids=true, to_apply=%add.2 | all-reduce | flops 32 | bytes 256
  50.3 0.7 dynamic_slice.6
  50.9 0.7 and_select_fusion.6
  51.7 0.7 add_compare_fusion
  53.0 9.2 %scatter_custom_fusion = s32[1152]{0:T(1024)S(1)} fusion(s32[1152]{0:T(1024)S(1)} %fusion.21, s32[1152]{0:T(1024)S(1)} %broadcast.571, s32[]{:T(128)} %constant.140.clone.1), kind=kCustom, calls=%fused_computation.112 | custom fusion | flops 1152 | bytes 4612 | tf_op jit(solution)/shard_map/scatter-add | solution.py:81
  62.8 0.8 fusion.17
  63.7 6.5 %gather_fusion = s32[1152]{0:T(1024)S(1)} fusion(s32[1152]{0:T(1024)S(1)} %fusion.17, s32[2048]{0:T(1024)S(1)} %pad_clamp_fusion.3), kind=kCustom, calls=%fused_computation | custom fusion | bytes 13824 | tf_op jit(solution)/shard_map/gather | solution.py:87
  70.3 1.6 pad_maximum_fusion.19
  72.0 0.5 collective-permute-start.2
  72.8 0.4 broadcast_maximum_fusion
  73.2 5.7 %broadcast_in_dim.87 = f32[25,48,12,66]{3,2,1,0:T(8,128)} broadcast(f32[25,48,12]{2,1,0:T(8,128)S(1)} %broadcast_minimum_fusion), dimensions={0,1,2} | broadcast | bytes 3859200 | tf_op jit(solution)/shard_map/broadcast_in_dim | solution.py:49
  78.9 9.2 %min.15 = f32[25,48,792]{2,1,0:T(8,128)} reshape(f32[25,48,12,66]{3,2,1,0:T(8,128)} %broadcast_in_dim.87) | data formatting | bytes 7603200 | tf_op jit(solution)/shard_map/min | solution.py:50
  88.1 5.7 %broadcast_in_dim.86 = f32[25,48,12,66]{3,2,1,0:T(8,128)} broadcast(f32[25,48,12]{2,1,0:T(8,128)S(1)} %get-tuple-element.23), dimensions={0,1,2} | broadcast | bytes 3859200 | tf_op jit(solution)/shard_map/broadcast_in_dim | solution.py:49
  93.8 9.2 %max.26 = f32[25,48,792]{2,1,0:T(8,128)} reshape(f32[25,48,12,66]{3,2,1,0:T(8,128)} %broadcast_in_dim.86) | data formatting | bytes 7603200 | tf_op jit(solution)/shard_map/max | solution.py:50
  103.0 8.9 %fusion.4 = f32[25,48,792]{2,1,0:T(8,128)} fusion(f32[25,48,792]{2,1,0:T(8,128)} %min.15, f32[1,48,816]{2,1,0:T(8,128)S(1)} %collective-permute-done.1, f32[24,48,24]{2,1,0:T(8,128)S(1)} %copy.91, f32[24,48,792]{2,1,0:T(8,128)} %param.5, f32[25,48,792]{2,1,0:T(8,128)} %max.26, f32[1,48,816]{2,1,0:T(8,128)S(1)} %collective-permute-done), kind=kLoop, calls=%fused_computation.21 | loop fusion | flops 6652800 | bytes 15478272 | tf_op jit(solution)/shard_map/add | solution.py:50
  111.9 0.8 pad_maximum_fusion.12
  113.7 5.6 %broadcast_in_dim.89 = f32[24,49,12,66]{3,2,0,1:T(8,128)} broadcast(f32[24,49,12]{2,0,1:T(8,128)S(1)} %copy.96), dimensions={0,1,2} | broadcast | bytes 3782016 | tf_op jit(solution)/shard_map/broadcast_in_dim | solution.py:52
  119.3 9.1 %min.17 = f32[24,49,792]{2,0,1:T(8,128)} reshape(f32[24,49,12,66]{3,2,0,1:T(8,128)} %broadcast_in_dim.89) | data formatting | bytes 7451136 | tf_op jit(solution)/shard_map/min | solution.py:53
  128.7 5.6 %broadcast_in_dim.88 = f32[24,49,12,66]{3,2,0,1:T(8,128)} broadcast(f32[24,49,12]{2,0,1:T(8,128)S(1)} %copy.94), dimensions={0,1,2} | broadcast | bytes 3782016 | tf_op jit(solution)/shard_map/broadcast_in_dim | solution.py:52
  134.3 9.1 %max.28 = f32[24,49,792]{2,0,1:T(8,128)} reshape(f32[24,49,12,66]{3,2,0,1:T(8,128)} %broadcast_in_dim.88) | data formatting | bytes 7451136 | tf_op jit(solution)/shard_map/max | solution.py:53
  143.4 8.6 %fusion.1 = f32[24,49,792]{2,1,0:T(8,128)S(1)} fusion(f32[26,1,816]{2,1,0:T(1,128)S(1)} %collective-permute-done.3, f32[1,48,816]{2,1,0:T(8,128)S(1)} %collective-permute-done.1, f32[1,48,816]{2,1,0:T(8,128)S(1)} %collective-permute-done, f32[24,48,24]{2,1,0:T(8,128)S(1)} %copy.91, f32[24,48,792]{2,1,0:T(8,128)} %param.5, ...), kind=kLoop, calls=%fused_computation.10 | loop fusion | flops 10245312 | bytes 15419904 | tf_op jit(solution)/shard_map/add | solution.py:53
  152.0 5.4 %fusion.36 = (bf16[24,48,792]{2,1,0:T(8,128)(2,1)S(1)}, f32[24,48,792]{2,1,0:T(8,128)}) fusion(f32[24,49,792]{2,1,0:T(8,128)S(1)} %fusion.1, f32[24,48,792]{2,1,0:T(8,128)S(1)} %copy-done.2, f32[25,48,792]{2,1,0:T(8,128)} %fusion.4), kind=kLoop, calls=%fused_computation.134 | loop fusion | flops 4561920 | bytes 23721984 | tf_op jit(solution)/shard_map/convert_element_type | solution.py:69
  157.4 4.9 %gather_fusion.1 = bf16[1152,792]{1,0:T(8,128)(2,1)} fusion(bf16[1152,792]{1,0:T(8,128)(2,1)S(1)} %bitcast.67, s32[2048]{0:T(1024)S(1)} %pad_clamp_fusion.2), kind=kCustom, calls=%fused_computation.1 | custom fusion | bytes 3654144 | tf_op jit(solution)/shard_map/gather | solution.py:87
  162.3 3.9 %copy_select_fusion = bf16[36,32,792]{2,0,1:T(8,128)(2,1)} fusion(bf16[36,32,792]{2,1,0:T(8,128)(2,1)} %bitcast.70, pred[36,32]{0,1:T(8,128)(4,1)S(1)} %copy.99), kind=kLoop, calls=%fused_computation.32 | loop fusion | flops 912384 | bytes 3650688 | tf_op jit(solution)/shard_map/jit(_where)/select_n | solution.py:86
  166.2 5.9 %all-to-all-start = ((bf16[36,32,792]{2,0,1:T(8,128)(2,1)}), bf16[36,32,792]{2,0,1:T(8,128)(2,1)S(1)}, u32[]{:S(2)}, u32[]{:S(2)}) async-start(bf16[36,32,792]{2,0,1:T(8,128)(2,1)} %copy_select_fusion), calls=%async_computation | async-start | bytes 4587520 | tf_op jit(solution)/shard_map/all_to_all | solution.py:98
  172.2 1.6 gather_fusion.2
  173.8 0.4 convolution_compare_fusion
  174.6 0.9 broadcast_select_fusion
  175.6 49.4 %all-to-all-done = bf16[36,32,792]{2,0,1:T(8,128)(2,1)S(1)} async-done(((bf16[36,32,792]{2,0,1:T(8,128)(2,1)}), bf16[36,32,792]{2,0,1:T(8,128)(2,1)S(1)}, u32[]{:S(2)}, u32[]{:S(2)}) %all-to-all-start) | async-done | bytes 1824800 | tf_op jit(solution)/shard_map/all_to_all | solution.py:98
  224.9 1.6 copy.101
  226.5 2.9 gather_fusion.3
  229.5 0.4 reshape.600
  230.2 6.1 %multiply_convert_fusion = bf16[1728,66,66]{0,2,1:T(8,128)(2,1)} fusion(f32[1728,66]{0,1:T(8,128)S(1)} %copy.102), kind=kLoop, calls=%fused_computation.7 | loop fusion | flops 15054336 | bytes 15510528 | tf_op jit(solution)/shard_map/while/body/eval_jaxpr/convert_element_type | solution.py:31
  236.3 20.8 %convert_element_type.60 = bf16[1728,4356]{0,1:T(8,128)(2,1)} reshape(bf16[1728,66,66]{0,2,1:T(8,128)(2,1)} %multiply_convert_fusion) | data formatting | bytes 30108672 | tf_op jit(solution)/shard_map/while/body/eval_jaxpr/convert_element_type | solution.py:31
  257.1 7.7 %fusion.9 = bf16[1728,128]{0,1:T(8,128)(2,1)S(1)} fusion(bf16[1728,4356]{0,1:T(8,128)(2,1)} %convert_element_type.60, bf16[4356,66]{0,1:T(8,128)(2,1)S(1)} %copy-done.4), kind=kOutput, calls=%fused_computation.33 | convolution fusion | flops 1926955008 | bytes 16071696 | tf_op jit(solution)/shard_map/while/body/eval_jaxpr/dot_general | solution.py:32
  265.5 4.7 %gather_fusion.4 = bf16[1152,792]{1,0:T(8,128)(2,1)S(1)} fusion(bf16[145,792]{1,0:T(8,128)(2,1)S(1)} %concatenate.36, s32[2048]{0:T(1024)S(1)} %pad_clamp_fusion.1), kind=kCustom, calls=%fused_computation.4 | custom fusion | bytes 3654144 | tf_op jit(solution)/shard_map/gather | solution.py:103
  270.2 2.0 copy.105
  272.3 4.3 %all-to-all-start.1 = ((bf16[36,32,792]{2,0,1:T(8,128)(2,1)}), bf16[36,32,792]{2,0,1:T(8,128)(2,1)}, u32[]{:S(2)}, u32[]{:S(2)}) async-start(bf16[36,32,792]{2,0,1:T(8,128)(2,1)} %copy.105), calls=%async_computation.1 | async-start | bytes 4587520 | tf_op jit(solution)/shard_map/all_to_all | solution.py:102
  277.2 0.7 fusion.25
  278.0 51.6 %all-to-all-done.1 = bf16[36,32,792]{2,0,1:T(8,128)(2,1)} async-done(((bf16[36,32,792]{2,0,1:T(8,128)(2,1)}), bf16[36,32,792]{2,0,1:T(8,128)(2,1)}, u32[]{:S(2)}, u32[]{:S(2)}) %all-to-all-start.1) | async-done | bytes 1824800 | tf_op jit(solution)/shard_map/all_to_all | solution.py:102
  329.6 1.9 copy.106
  331.5 4.9 %gather_fusion.5 = bf16[1152,792]{1,0:T(8,128)(2,1)} fusion(bf16[1152,792]{1,0:T(8,128)(2,1)S(1)} %bitcast.68, s32[2048]{0:T(1024)S(1)} %pad_clamp_fusion), kind=kCustom, calls=%fused_computation.5 | custom fusion | bytes 3654144 | tf_op jit(solution)/shard_map/gather | solution.py:112
  336.4 5.3 %fusion.8 = f32[24,48,792]{2,1,0:T(8,128)} fusion(f32[24,48,792]{2,1,0:T(8,128)} %get-tuple-element.22, bf16[24,48,792]{2,1,0:T(8,128)(2,1)} %bitcast.72, pred[24,48]{1,0:T(8,128)(4,1)S(1)} %broadcast_compare_fusion.1), kind=kLoop, calls=%fused_computation.31 | loop fusion | flops 2737152 | bytes 9124992 | tf_op jit(solution)/shard_map/add | solution.py:113
  (77 shorter events, 5.7 us)
Async XLA Ops:
  0.0 8.3 %copy-start.5 = (s32[24,48]{1,0:T(8,128)S(1)}, s32[24,48]{1,0:T(8,128)}, u32[]{:S(2)}) copy-start(s32[24,48]{1,0:T(8,128)} %param.7) | copy-start | bytes 13828
  2.3 68.0 %collective-permute-start.1 = (f32[1,48,816]{2,1,0:T(8,128)S(1)}, f32[1,48,816]{2,1,0:T(8,128)S(1)}, u32[]{:S(2)}, u32[]{:S(2)}) collective-permute-start(f32[1,48,816]{2,1,0:T(8,128)S(1)} %get-tuple-element.30), channel_id=1, source_target_pairs={{4,0},{8,4},{12,8},{16,12},{20,16},{24,20},{28,24},{0,28},{5,1},{9... | collective-permute-start | bytes 470024 | tf_op jit(solution)/shard_map/ppermute | solution.py:17
  8.3 61.9 %collective-permute-start = (f32[1,48,816]{2,1,0:T(8,128)S(1)}, f32[1,48,816]{2,1,0:T(8,128)S(1)}, u32[]{:S(2)}, u32[]{:S(2)}) collective-permute-start(f32[1,48,816]{2,1,0:T(8,128)S(1)} %get-tuple-element.29), channel_id=1, source_target_pairs={{0,4},{4,8},{8,12},{12,16},{16,20},{20,24},{24,28},{28,0},{1,5},{5... | collective-permute-start | bytes 470024 | tf_op jit(solution)/shard_map/ppermute | solution.py:16
  70.2 2.6 copy-start
  71.9 40.0 %collective-permute-start.3 = (f32[26,1,816]{2,1,0:T(1,128)S(1)}, f32[26,1,816]{2,1,0:T(1,128)S(1)}, u32[]{:S(2)}, u32[]{:S(2)}) collective-permute-start(f32[26,1,816]{2,1,0:T(1,128)S(1)} %get-tuple-element.28), channel_id=1, source_target_pairs={{1,0},{2,1},{3,2},{0,3},{5,4},{6,5},{7,6},{4,7},{9,8},{10,9},{11,1... | collective-permute-start | bytes 254600 | tf_op jit(solution)/shard_map/ppermute | solution.py:17
  72.0 39.9 %collective-permute-start.2 = (f32[26,1,816]{2,1,0:T(1,128)S(1)}, f32[26,1,816]{2,1,0:T(1,128)S(1)}, u32[]{:S(2)}, u32[]{:S(2)}) collective-permute-start(f32[26,1,816]{2,1,0:T(1,128)S(1)} %get-tuple-element.27), channel_id=1, source_target_pairs={{0,1},{1,2},{2,3},{3,0},{4,5},{5,6},{6,7},{7,4},{8,9},{9,10},{10,1... | collective-permute-start | bytes 254600 | tf_op jit(solution)/shard_map/ppermute | solution.py:16
  103.0 8.9 %copy-start.1 = (f32[24,48,792]{2,1,0:T(8,128)S(1)}, f32[24,48,792]{2,1,0:T(8,128)}, u32[]{:S(2)}) copy-start(f32[24,48,792]{2,1,0:T(8,128)} %param.5) | copy-start | bytes 10948612
  143.4 8.6 %copy-start.2 = (f32[24,48,792]{2,1,0:T(8,128)S(1)}, f32[24,48,792]{2,1,0:T(8,128)}, u32[]{:S(2)}) copy-start(f32[24,48,792]{2,1,0:T(8,128)} %param.5) | copy-start | bytes 10948612
  162.3 11.5 %copy-start.6 = (s32[6,6]{1,0:T(8,128)S(1)}, s32[6,6]{1,0:T(8,128)}, u32[]{:S(2)}) copy-start(s32[6,6]{1,0:T(8,128)} %param.9) | copy-start | bytes 436
  162.3 12.3 %copy-start.3 = (bf16[4356,66]{0,1:T(8,128)(2,1)S(1)}, bf16[4356,66]{0,1:T(8,128)(2,1)}, u32[]{:S(2)}) copy-start(bf16[4356,66]{0,1:T(8,128)(2,1)} %param.8) | copy-start | bytes 1724980
  166.2 58.7 %all-to-all-start = ((bf16[36,32,792]{2,0,1:T(8,128)(2,1)}), bf16[36,32,792]{2,0,1:T(8,128)(2,1)S(1)}, u32[]{:S(2)}, u32[]{:S(2)}) async-start(bf16[36,32,792]{2,0,1:T(8,128)(2,1)} %copy_select_fusion), calls=%async_computation | async-start | bytes 4587520 | tf_op jit(solution)/shard_map/all_to_all | solution.py:98
  236.3 20.8 %copy-start.4 = (bf16[4356,66]{0,1:T(8,128)(2,1)S(1)}, bf16[4356,66]{0,1:T(8,128)(2,1)}, u32[]{:S(2)}) copy-start(bf16[4356,66]{0,1:T(8,128)(2,1)} %broadcast_select_fusion) | copy-start | bytes 1724980
  272.3 57.3 %all-to-all-start.1 = ((bf16[36,32,792]{2,0,1:T(8,128)(2,1)}), bf16[36,32,792]{2,0,1:T(8,128)(2,1)}, u32[]{:S(2)}, u32[]{:S(2)}) async-start(bf16[36,32,792]{2,0,1:T(8,128)(2,1)} %copy.105), calls=%async_computation.1 | async-start | bytes 4587520 | tf_op jit(solution)/shard_map/all_to_all | solution.py:102
where the time goes:
time: 343 us; the launch traced here: 342 us
  local copies, waits for them, and re-layouts  118 us (34%)
  waiting for transfers between devices  101 us (29%)
  other arithmetic  57.7 us (17%)
  blocking collectives  40.1 us (12%)
  starting transfers between devices  16.7 us (5%)
  matrix products  8.16 us (2%)
    all_to_all x1, waiting for transfers between devices, per_device(): lax.all_to_all(extended[slot_of.reshape(-1)].reshape(send_rows, devices,...  51.6 us
    all_to_all x1, waiting for transfers between devices, per_device(): lax.all_to_all(outgoing, ('gx', 'gy'), split_axis=1, concat_axis=1, tiled...  49.4 us
    unnamed x1, blocking collectives  40.1 us
    convert_element_type x1, local copies, waits for them, and re-layouts, one_block(): (wide[:, :, None] * wide[:, None, :]).astype(jnp.bfloat16)  20.8 us
    broadcast_in_dim x2, local copies, waits for them, and re-layouts, per_device(): jnp.repeat(0.5 * (wind_x[:-1, 1:-1] + wind_x[1:, 1:-1]), chan, axis=2)  11.3 us
    broadcast_in_dim x2, local copies, waits for them, and re-layouts, per_device(): jnp.repeat(0.5 * (wind_y[1:-1, :-1] + wind_y[1:-1, 1:]), chan, axis=2)  11.2 us
    max x2, local copies, waits for them, and re-layouts, per_device(): jnp.maximum(face_y, 0.0) * along_y[:, :-1]  9.41 us
    min x2, local copies, waits for them, and re-layouts, per_device(): jnp.minimum(face_y, 0.0) * along_y[:, 1:]  9.41 us
  transfers between devices with their start and end apart: 6, of which 2 were waited for; matrix products, arithmetic and copies ran while one was open for 19% of the time, Pallas kernels for 0%

commit v1 on v0

--- a/solution.py
+++ b/solution.py
@@ -4,6 +4,12 @@
 from jax.sharding import PartitionSpec as P
 
 BLK = 11
+
+
+def exchange_blocks(x, name, split, join):
+    pieces = jnp.split(x, lax.axis_size(name), axis=split)
+    arrived = lax.all_to_all(jnp.stack(pieces), name, 0, 0)
+    return jnp.concatenate(arrived, axis=join)
 
 
 def padded_2(array, sides, width):
@@ -95,7 +101,7 @@
     source_dev = jnp.sum((ends[None, :] <= global_rank[:, None]).astype(jnp.int32), axis=1)
     local_rank = global_rank - starts[source_dev]
     arrive_row = local_rank // devices * devices + source_dev
-    arrived = lax.all_to_all(outgoing, ("gx", "gy"), split_axis=1, concat_axis=1, tiled=True)
+    arrived = exchange_blocks(outgoing, ("gx", "gy"), 1, 1)
     gathered = arrived.reshape(send_rows * devices, width)[arrive_row]
     computed = coalesce(gathered, chan, kernel_wide)
     extended = jnp.concatenate([computed, jnp.zeros((1, width), jnp.bfloat16)], axis=0)

time: 343 us -> 362 us (1.055)
  local copies, waits for them, and re-layouts: 118 us -> 138 us
    unnamed x19 -> x50, local copies, waits for them, and re-layouts: 2.91 us -> 22.5 us
  transfers between devices with their start and end apart: 6 -> 6, of which waited for: 2 -> 2; matrix products, arithmetic and copies ran while one was open for 19% -> 18% of each run, Pallas kernels for 0% -> 0%
where the time goes in v1:
time: 362 us; the launch traced here: 361 us
  local copies, waits for them, and re-layouts  138 us (38%)
  waiting for transfers between devices  101 us (28%)
  other arithmetic  56.3 us (16%)
  blocking collectives  40.1 us (11%)
  starting transfers between devices  16.7 us (5%)
  matrix products  8.16 us (2%)
    all_to_all x1, waiting for transfers between devices, per_device(): lax.all_to_all(extended[slot_of.reshape(-1)].reshape(send_rows, devices,...  51.6 us
    all_to_all x1, waiting for transfers between devices, exchange_blocks(): arrived = lax.all_to_all(jnp.stack(pieces), name, 0, 0)  49.6 us
    unnamed x1, blocking collectives  40.1 us
    unnamed x50, local copies, waits for them, and re-layouts  22.5 us
    convert_element_type x1, local copies, waits for them, and re-layouts, one_block(): (wide[:, :, None] * wide[:, None, :]).astype(jnp.bfloat16)  20.8 us
    broadcast_in_dim x2, local copies, waits for them, and re-layouts, per_device(): jnp.repeat(0.5 * (wind_x[:-1, 1:-1] + wind_x[1:, 1:-1]), chan, axis=2)  11.3 us
    broadcast_in_dim x2, local copies, waits for them, and re-layouts, per_device(): jnp.repeat(0.5 * (wind_y[1:-1, :-1] + wind_y[1:-1, 1:]), chan, axis=2)  11.2 us
    max x2, local copies, waits for them, and re-layouts, per_device(): jnp.maximum(face_y, 0.0) * along_y[:, :-1]  9.41 us
  transfers between devices with their start and end apart: 6, of which 2 were waited for; matrix products, arithmetic and copies ran while one was open for 18% of the time, Pallas kernels for 0%

profile of v1, /device:TPU:0, one launch (start us, length us, event | category | flops | bytes accessed | tf_op | source)
XLA Modules:
  0.0 360.8 jit_solution(12253043980687756776)
XLA Ops:
  0.0 1.2 copy.126
  1.2 1.1 pad_maximum_fusion.15
  2.3 6.0 %collective-permute-start.1 = (f32[1,48,816]{2,1,0:T(8,128)S(1)}, f32[1,48,816]{2,1,0:T(8,128)S(1)}, u32[]{:S(2)}, u32[]{:S(2)}) collective-permute-start(f32[1,48,816]{2,1,0:T(8,128)S(1)} %get-tuple-element.30), channel_id=1, source_target_pairs={{4,0},{8,4},{12,8},{16,12},{20,16},{24,20},{28,24},{0,28},{5,1},{9... | collective-permute-start | bytes 470024 | tf_op jit(solution)/shard_map/ppermute | solution.py:23
  8.3 0.7 fusion.67
  9.1 0.8 dynamic-update-slice
  9.8 40.1 %all-reduce.2 = s32[32]{0:T(128)S(1)} all-reduce(s32[32]{0:T(128)S(1)} %dynamic-update-slice), channel_id=1, replica_groups=mesh['gx'=8,'gy'=4] {'gx','gy'}, use_global_device_ids=true, to_apply=%add.2 | all-reduce | flops 32 | bytes 256
  50.2 0.7 dynamic_slice.6
  50.8 0.7 and_select_fusion.6
  51.5 0.7 add_compare_fusion
  53.2 9.2 %scatter_custom_fusion = s32[1152]{0:T(1024)S(1)} fusion(s32[1152]{0:T(1024)S(1)} %fusion.53, s32[1152]{0:T(1024)S(1)} %broadcast.571, s32[]{:T(128)} %constant.140.clone.1), kind=kCustom, calls=%fused_computation.176 | custom fusion | flops 1152 | bytes 4612 | tf_op jit(solution)/shard_map/scatter-add | solution.py:87
  63.1 0.8 fusion.49
  64.0 6.5 %gather_fusion = s32[1152]{0:T(1024)S(1)} fusion(s32[1152]{0:T(1024)S(1)} %fusion.49, s32[2048]{0:T(1024)S(1)} %pad_clamp_fusion.3), kind=kCustom, calls=%fused_computation | custom fusion | bytes 13824 | tf_op jit(solution)/shard_map/gather | solution.py:93
  70.5 1.6 pad_maximum_fusion.19
  73.5 5.7 %broadcast_in_dim.87 = f32[25,48,12,66]{3,2,1,0:T(8,128)} broadcast(f32[25,48,12]{2,1,0:T(8,128)S(1)} %broadcast_minimum_fusion), dimensions={0,1,2} | broadcast | bytes 3859200 | tf_op jit(solution)/shard_map/broadcast_in_dim | solution.py:55
  79.2 9.2 %min.15 = f32[25,48,792]{2,1,0:T(8,128)} reshape(f32[25,48,12,66]{3,2,1,0:T(8,128)} %broadcast_in_dim.87) | data formatting | bytes 7603200 | tf_op jit(solution)/shard_map/min | solution.py:56
  88.4 5.7 %broadcast_in_dim.86 = f32[25,48,12,66]{3,2,1,0:T(8,128)} broadcast(f32[25,48,12]{2,1,0:T(8,128)S(1)} %get-tuple-element.23), dimensions={0,1,2} | broadcast | bytes 3859200 | tf_op jit(solution)/shard_map/broadcast_in_dim | solution.py:55
  94.0 9.2 %max.26 = f32[25,48,792]{2,1,0:T(8,128)} reshape(f32[25,48,12,66]{3,2,1,0:T(8,128)} %broadcast_in_dim.86) | data formatting | bytes 7603200 | tf_op jit(solution)/shard_map/max | solution.py:56
  103.3 8.9 %fusion.4 = f32[25,48,792]{2,1,0:T(8,128)} fusion(f32[25,48,792]{2,1,0:T(8,128)} %min.15, f32[1,48,816]{2,1,0:T(8,128)S(1)} %collective-permute-done.1, f32[24,48,24]{2,1,0:T(8,128)S(1)} %copy.126, f32[24,48,792]{2,1,0:T(8,128)} %param.5, f32[25,48,792]{2,1,0:T(8,128)} %max.26, f32[1,48,816]{2,1,0:T(8,128)S(1)} %collective-permute-done), kind=kLoop, calls=%fused_computation.21 | loop fusion | flops 6652800 | bytes 15478272 | tf_op jit(solution)/shard_map/add | solution.py:56
  112.2 0.8 pad_maximum_fusion.12
  114.0 5.6 %broadcast_in_dim.89 = f32[24,49,12,66]{3,2,0,1:T(8,128)} broadcast(f32[24,49,12]{2,0,1:T(8,128)S(1)} %copy.131), dimensions={0,1,2} | broadcast | bytes 3782016 | tf_op jit(solution)/shard_map/broadcast_in_dim | solution.py:58
  119.6 9.1 %min.17 = f32[24,49,792]{2,0,1:T(8,128)} reshape(f32[24,49,12,66]{3,2,0,1:T(8,128)} %broadcast_in_dim.89) | data formatting | bytes 7451136 | tf_op jit(solution)/shard_map/min | solution.py:59
  129.0 5.6 %broadcast_in_dim.88 = f32[24,49,12,66]{3,2,0,1:T(8,128)} broadcast(f32[24,49,12]{2,0,1:T(8,128)S(1)} %copy.129), dimensions={0,1,2} | broadcast | bytes 3782016 | tf_op jit(solution)/shard_map/broadcast_in_dim | solution.py:58
  134.6 9.1 %max.28 = f32[24,49,792]{2,0,1:T(8,128)} reshape(f32[24,49,12,66]{3,2,0,1:T(8,128)} %broadcast_in_dim.88) | data formatting | bytes 7451136 | tf_op jit(solution)/shard_map/max | solution.py:59
  143.7 8.6 %fusion.1 = f32[24,49,792]{2,1,0:T(8,128)S(1)} fusion(f32[26,1,816]{2,1,0:T(1,128)S(1)} %collective-permute-done.3, f32[1,48,816]{2,1,0:T(8,128)S(1)} %collective-permute-done.1, f32[1,48,816]{2,1,0:T(8,128)S(1)} %collective-permute-done, f32[24,48,24]{2,1,0:T(8,128)S(1)} %copy.126, f32[24,48,792]{2,1,0:T(8,128)} %param.5, ...), kind=kLoop, calls=%fused_computation.10 | loop fusion | flops 10245312 | bytes 15419904 | tf_op jit(solution)/shard_map/add | solution.py:59
  152.3 5.4 %fusion.68 = (bf16[24,48,792]{2,1,0:T(8,128)(2,1)S(1)}, f32[24,48,792]{2,1,0:T(8,128)}) fusion(f32[24,49,792]{2,1,0:T(8,128)S(1)} %fusion.1, f32[24,48,792]{2,1,0:T(8,128)S(1)} %copy-done.2, f32[25,48,792]{2,1,0:T(8,128)} %fusion.4), kind=kLoop, calls=%fused_computation.198 | loop fusion | flops 4561920 | bytes 23721984 | tf_op jit(solution)/shard_map/convert_element_type | solution.py:75
  157.8 4.9 %gather_fusion.1 = bf16[1152,792]{1,0:T(8,128)(2,1)} fusion(bf16[1152,792]{1,0:T(8,128)(2,1)S(1)} %bitcast.196, s32[2048]{0:T(1024)S(1)} %get-tuple-element.40), kind=kCustom, calls=%fused_computation.1 | custom fusion | bytes 3654144 | tf_op jit(solution)/shard_map/gather | solution.py:93
  162.7 2.5 copy_select_fusion
  166.4 0.6 fusion.43
  180.9 0.6 fusion.20
  182.2 0.6 fusion.18
  184.1 0.6 fusion.15
  185.4 5.8 %all-to-all-start = ((bf16[32,36,1,792]{3,1,2,0:T(8,128)(2,1)}), bf16[32,36,1,792]{3,1,2,0:T(8,128)(2,1)S(1)}, u32[]{:S(2)}, u32[]{:S(2)}) async-start(bf16[32,36,1,792]{3,1,2,0:T(8,128)(2,1)} %fusion.14), calls=%async_computation | async-start | bytes 4587520 | tf_op jit(solution)/shard_map/all_to_all | solution.py:11
  191.3 1.6 gather_fusion.2
  193.5 0.9 broadcast_select_fusion
  194.4 49.6 %all-to-all-done = bf16[32,36,1,792]{3,1,2,0:T(8,128)(2,1)S(1)} async-done(((bf16[32,36,1,792]{3,1,2,0:T(8,128)(2,1)}), bf16[32,36,1,792]{3,1,2,0:T(8,128)(2,1)S(1)}, u32[]{:S(2)}, u32[]{:S(2)}) %all-to-all-start) | async-done | bytes 1824800 | tf_op jit(solution)/shard_map/all_to_all | solution.py:11
  244.0 1.6 copy.136
  245.6 2.9 gather_fusion.3
  249.3 6.1 %multiply_convert_fusion = bf16[1728,66,66]{0,2,1:T(8,128)(2,1)} fusion(f32[1728,66]{0,1:T(8,128)S(1)} %copy.137), kind=kLoop, calls=%fused_computation.7 | loop fusion | flops 15054336 | bytes 15510528 | tf_op jit(solution)/shard_map/while/body/eval_jaxpr/convert_element_type | solution.py:37
  255.4 20.8 %convert_element_type.60 = bf16[1728,4356]{0,1:T(8,128)(2,1)} reshape(bf16[1728,66,66]{0,2,1:T(8,128)(2,1)} %multiply_convert_fusion) | data formatting | bytes 30108672 | tf_op jit(solution)/shard_map/while/body/eval_jaxpr/convert_element_type | solution.py:37
  276.2 7.7 %fusion.9 = bf16[1728,128]{0,1:T(8,128)(2,1)S(1)} fusion(bf16[1728,4356]{0,1:T(8,128)(2,1)} %convert_element_type.60, bf16[4356,66]{0,1:T(8,128)(2,1)S(1)} %copy-done.4), kind=kOutput, calls=%fused_computation.33 | convolution fusion | flops 1926955008 | bytes 16071696 | tf_op jit(solution)/shard_map/while/body/eval_jaxpr/dot_general | solution.py:38
  284.6 4.7 %gather_fusion.4 = bf16[1152,792]{1,0:T(8,128)(2,1)S(1)} fusion(bf16[145,792]{1,0:T(8,128)(2,1)S(1)} %concatenate.36, s32[2048]{0:T(1024)S(1)} %get-tuple-element.39), kind=kCustom, calls=%fused_computation.4 | custom fusion | bytes 3654144 | tf_op jit(solution)/shard_map/gather | solution.py:109
  289.3 2.0 copy.140
  291.4 4.3 %all-to-all-start.1 = ((bf16[36,32,792]{2,0,1:T(8,128)(2,1)}), bf16[36,32,792]{2,0,1:T(8,128)(2,1)}, u32[]{:S(2)}, u32[]{:S(2)}) async-start(bf16[36,32,792]{2,0,1:T(8,128)(2,1)} %copy.140), calls=%async_computation.1 | async-start | bytes 4587520 | tf_op jit(solution)/shard_map/all_to_all | solution.py:108
  296.3 0.7 fusion.57
  297.1 51.6 %all-to-all-done.1 = bf16[36,32,792]{2,0,1:T(8,128)(2,1)} async-done(((bf16[36,32,792]{2,0,1:T(8,128)(2,1)}), bf16[36,32,792]{2,0,1:T(8,128)(2,1)}, u32[]{:S(2)}, u32[]{:S(2)}) %all-to-all-start.1) | async-done | bytes 1824800 | tf_op jit(solution)/shard_map/all_to_all | solution.py:108
  348.7 1.9 copy.141
  350.6 4.9 %gather_fusion.5 = bf16[1152,792]{1,0:T(8,128)(2,1)} fusion(bf16[1152,792]{1,0:T(8,128)(2,1)S(1)} %bitcast.197, s32[2048]{0:T(1024)S(1)} %pad_clamp_fusion), kind=kCustom, calls=%fused_computation.5 | custom fusion | bytes 3654144 | tf_op jit(solution)/shard_map/gather | solution.py:118
  355.5 5.3 %fusion.8 = f32[24,48,792]{2,1,0:T(8,128)} fusion(f32[24,48,792]{2,1,0:T(8,128)} %get-tuple-element.22, bf16[24,48,792]{2,1,0:T(8,128)(2,1)} %bitcast.202, pred[24,48]{1,0:T(8,128)(4,1)S(1)} %broadcast_compare_fusion.1), kind=kLoop, calls=%fused_computation.31 | loop fusion | flops 2737152 | bytes 9124992 | tf_op jit(solution)/shard_map/add | solution.py:119
  (108 shorter events, 25.1 us)
Async XLA Ops:
  1.2 7.1 %copy-start.5 = (s32[24,48]{1,0:T(8,128)S(1)}, s32[24,48]{1,0:T(8,128)}, u32[]{:S(2)}) copy-start(s32[24,48]{1,0:T(8,128)} %param.7) | copy-start | bytes 13828
  2.3 68.2 %collective-permute-start.1 = (f32[1,48,816]{2,1,0:T(8,128)S(1)}, f32[1,48,816]{2,1,0:T(8,128)S(1)}, u32[]{:S(2)}, u32[]{:S(2)}) collective-permute-start(f32[1,48,816]{2,1,0:T(8,128)S(1)} %get-tuple-element.30), channel_id=1, source_target_pairs={{4,0},{8,4},{12,8},{16,12},{20,16},{24,20},{28,24},{0,28},{5,1},{9... | collective-permute-start | bytes 470024 | tf_op jit(solution)/shard_map/ppermute | solution.py:23
  8.3 62.2 %collective-permute-start = (f32[1,48,816]{2,1,0:T(8,128)S(1)}, f32[1,48,816]{2,1,0:T(8,128)S(1)}, u32[]{:S(2)}, u32[]{:S(2)}) collective-permute-start(f32[1,48,816]{2,1,0:T(8,128)S(1)} %get-tuple-element.29), channel_id=1, source_target_pairs={{0,4},{4,8},{8,12},{12,16},{16,20},{20,24},{24,28},{28,0},{1,5},{5... | collective-permute-start | bytes 470024 | tf_op jit(solution)/shard_map/ppermute | solution.py:22
  70.5 2.6 copy-start
  72.2 40.0 %collective-permute-start.3 = (f32[26,1,816]{2,1,0:T(1,128)S(1)}, f32[26,1,816]{2,1,0:T(1,128)S(1)}, u32[]{:S(2)}, u32[]{:S(2)}) collective-permute-start(f32[26,1,816]{2,1,0:T(1,128)S(1)} %get-tuple-element.28), channel_id=1, source_target_pairs={{1,0},{2,1},{3,2},{0,3},{5,4},{6,5},{7,6},{4,7},{9,8},{10,9},{11,1... | collective-permute-start | bytes 254600 | tf_op jit(solution)/shard_map/ppermute | solution.py:23
  72.2 39.9 %collective-permute-start.2 = (f32[26,1,816]{2,1,0:T(1,128)S(1)}, f32[26,1,816]{2,1,0:T(1,128)S(1)}, u32[]{:S(2)}, u32[]{:S(2)}) collective-permute-start(f32[26,1,816]{2,1,0:T(1,128)S(1)} %get-tuple-element.27), channel_id=1, source_target_pairs={{0,1},{1,2},{2,3},{3,0},{4,5},{5,6},{6,7},{7,4},{8,9},{9,10},{10,1... | collective-permute-start | bytes 254600 | tf_op jit(solution)/shard_map/ppermute | solution.py:22
  103.3 8.9 %copy-start.1 = (f32[24,48,792]{2,1,0:T(8,128)S(1)}, f32[24,48,792]{2,1,0:T(8,128)}, u32[]{:S(2)}) copy-start(f32[24,48,792]{2,1,0:T(8,128)} %param.5) | copy-start | bytes 10948612
  143.7 8.7 %copy-start.2 = (f32[24,48,792]{2,1,0:T(8,128)S(1)}, f32[24,48,792]{2,1,0:T(8,128)}, u32[]{:S(2)}) copy-start(f32[24,48,792]{2,1,0:T(8,128)} %param.5) | copy-start | bytes 10948612
  185.3 7.5 %copy-start.6 = (s32[6,6]{1,0:T(8,128)S(1)}, s32[6,6]{1,0:T(8,128)}, u32[]{:S(2)}) copy-start(s32[6,6]{1,0:T(8,128)} %param.9) | copy-start | bytes 436
  185.3 8.1 %copy-start.3 = (bf16[4356,66]{0,1:T(8,128)(2,1)S(1)}, bf16[4356,66]{0,1:T(8,128)(2,1)}, u32[]{:S(2)}) copy-start(bf16[4356,66]{0,1:T(8,128)(2,1)} %param.8) | copy-start | bytes 1724980
  185.4 58.7 %all-to-all-start = ((bf16[32,36,1,792]{3,1,2,0:T(8,128)(2,1)}), bf16[32,36,1,792]{3,1,2,0:T(8,128)(2,1)S(1)}, u32[]{:S(2)}, u32[]{:S(2)}) async-start(bf16[32,36,1,792]{3,1,2,0:T(8,128)(2,1)} %fusion.14), calls=%async_computation | async-start | bytes 4587520 | tf_op jit(solution)/shard_map/all_to_all | solution.py:11
  255.4 20.8 %copy-start.4 = (bf16[4356,66]{0,1:T(8,128)(2,1)S(1)}, bf16[4356,66]{0,1:T(8,128)(2,1)}, u32[]{:S(2)}) copy-start(bf16[4356,66]{0,1:T(8,128)(2,1)} %broadcast_select_fusion) | copy-start | bytes 1724980
  291.4 57.3 %all-to-all-start.1 = ((bf16[36,32,792]{2,0,1:T(8,128)(2,1)}), bf16[36,32,792]{2,0,1:T(8,128)(2,1)}, u32[]{:S(2)}, u32[]{:S(2)}) async-start(bf16[36,32,792]{2,0,1:T(8,128)(2,1)} %copy.140), calls=%async_computation.1 | async-start | bytes 4587520 | tf_op jit(solution)/shard_map/all_to_all | solution.py:108
